TPU v7x, 256 devices: a whole 4x4x8 slice. The times are simulated.
256 devices in a mesh: tm: 8 (over y, core), mp: 4 (over z_lo), tok: 8 (over z_hi, x).
Axes of the slice: x: 4, y: 4, z: 8 (z_hi: 2, z_lo: 4; z = z_hi * 4 + z_lo), core: 2. Of those that a mesh axis runs over, the one named last changes fastest.
Arguments:
- features: bfloat16 [1024, 3584], P('tok'), may hold values from -6 to 6
- spike_mask: int32 [8, 1024, 3584], P('tm', 'tok'), may hold values 0 or 1
- gate_weight: bfloat16 [3584, 7168], P(('tm', 'tok'), 'mp'), may hold values from -0.09375 to 0.09375
- threshold: float32 [7168], P('mp'), may hold values from 0.5 to 2
Outputs:
- rates: float32 [1024, 7168], P('tok', 'mp')
- grad_threshold: float32 [7168], P('mp')
All inputs are finite; a program needn't handle non-finite values. No bound on the sum of `spike_mask` on one device may be relied on, other than what follows from the above.
Results may differ from a plain program's by a relative error of at most 0.00035.
Values may be sent and summed in bfloat16 or wider, within the bound.
No kernel may reach another device: no remote copies, remote signals or barrier semaphores. Data moves between devices by JAX's collectives and lax.ppermute only.
A program may use at most 64 MiB of HBM per device.

v0:
```python
import jax
import jax.numpy as jnp
from jax import lax
from jax.sharding import PartitionSpec as P

SHARP = 2.0


def passed_along(x, axis, by):
    peers = lax.axis_size(axis)
    pairs = [(i, i + by) for i in range(peers) if 0 <= i + by < peers]
    return lax.ppermute(x, axis, pairs)


def on_device(features, spike_mask, gate_weight, threshold):
    steps = lax.axis_size("tm")
    step_index = lax.axis_index("tm")
    tokens_all = features.shape[0] * lax.axis_size("tok")
    rows = features.shape[0]
    width = gate_weight.shape[1]
    driven = jnp.where(spike_mask[0] > 0, features, jnp.zeros_like(features))
    piece = lax.all_gather(gate_weight, ("tm", "tok"), axis=0, tiled=True)
    student = jnp.dot(driven, piece, preferred_element_type=jnp.float32)
    teacher = jnp.dot(features, piece, preferred_element_type=jnp.float32)
    current = 2.0 * student
    target = jax.nn.silu(teacher)
    blocks = 1
    size = rows // blocks
    turns = steps + blocks - 1

    def forward_turn(turn, carry):
        incoming, spikes = carry
        block = turn - step_index
        active = (block >= 0) & (block < blocks)
        rising = incoming + current
        fired = jax.nn.sigmoid(SHARP * (rising - threshold))
        leaving = rising - threshold * fired
        older = spikes
        spikes = jnp.where(active, fired, older)
        passed = passed_along(leaving, "tm", 1)
        return (passed, spikes)

    block_zero = jnp.zeros((size, width), jnp.float32)
    unused, spikes = lax.fori_loop(
        0, turns, forward_turn, (block_zero, jnp.zeros((rows, width), jnp.float32))
    )
    total = lax.psum(spikes, "tm")
    rates = threshold * total / steps
    error = (rates - target) / tokens_all

    def backward_turn(turn, carry):
        incoming, grad_sum = carry
        block = turn - (steps - 1 - step_index)
        active = (block >= 0) & (block < blocks)
        dspike = error * threshold / steps - threshold * incoming
        dwide = dspike * SHARP * spikes * (1.0 - spikes)
        term = jnp.sum(-dwide - spikes * incoming + error * spikes / steps, axis=0)
        grad_sum = grad_sum + jnp.where(active, term, jnp.zeros_like(term))
        passed = passed_along((incoming + dwide).astype(jnp.bfloat16), "tm", -1).astype(jnp.float32)
        return (passed, grad_sum)

    unused_cot, grad_local = lax.fori_loop(
        0, turns, backward_turn, (block_zero, jnp.zeros((width,), jnp.float32))
    )
    grad_threshold = lax.psum(grad_local, ("tm", "tok"))
    return (rates, grad_threshold)


def solution(mesh):
    return jax.shard_map(
        on_device,
        mesh=mesh,
        in_specs=(P("tok", None), P("tm", "tok", None), P(("tm", "tok"), "mp"), P("mp")),
        out_specs=(P("tok", "mp"), P("mp")),
        check_vma=False,
    )
```

profile of v0, /device:TPU:32, one launch (start us, length us, event | category | flops | bytes accessed | tf_op | source)
XLA Modules:
  0.0 676.2 jit_solution(10581541776726929995)
XLA Ops:
  8.0 140.1 %all-gather.2.cloned.1.call-done = bf16[3584,1792]{1,0:T(8,128)(2,1)} async-done(((bf16[56,1792]{1,0:T(8,128)(2,1)}), bf16[3584,1792]{1,0:T(8,128)(2,1)}) %all-gather.2.cloned.1.call-update) | async-done | bytes 12845072 | tf_op jit(solution)/shard_map/all_gather | solution.py:22
  148.0 7.4 %convolution_multiply_fusion = f32[128,1792]{1,0:T(8,128)S(1)} fusion(bf16[3584,1792]{1,0:T(8,128)(2,1)} %all-gather.2.cloned.1.call-done, bf16[128,3584]{1,0:T(8,128)(2,1)} %param.8, s32[1,128,3584]{2,1,0:T(8,128)} %param.9), kind=kOutput, calls=%fused_computation.8 | convolution fusion | flops 1645314048 | bytes 16515072 | tf_op jit(solution)/shard_map/dot_general | solution.py:23
  155.5 120.2 %while.34 = (s32[]{:T(128)}, f32[128,1792]{1,0:T(8,128)S(1)}, f32[128,1792]{1,0:T(8,128)S(1)}, f32[128,1792]{1,0:T(8,128)S(1)}, f32[1792]{0:T(1024)S(1)}, /*index=5*/s32[]{:T(128)}, s32[]{:T(128)}, s32[]{:T(128)}) while((s32[]{:T(128)}, f32[128,1792]{1,0:T(8,128)S(1)}, f32[128,1792]{1,0:T(8,128)S(1)}, f32[128,1792]{1,0:T(8,128)S(1)}, ...), condition=%wide.region_1.2_spmd.clone, body=%wide.region_0.1_spmd.clone.sunk | while | flops 2293767 | bytes 8264873 | solution.py:44
  155.5 1.5 select_select_fusion.2
  157.1 2.2 collective-permute-start
  159.3 2.2 collective-permute-done
  163.1 11.6 %collective-permute-start = (f32[128,1792]{1,0:T(8,128)}, f32[128,1792]{1,0:T(8,128)S(1)}, u32[]{:S(2)}, u32[]{:S(2)}) collective-permute-start(f32[128,1792]{1,0:T(8,128)} %get-tuple-element.455), channel_id=1, source_target_pairs={{0,32},{32,64},{64,96},{96,128},{128,160},{160,192},{192,224},{1,3... | collective-permute-start | bytes 2752520 | tf_op jit(solution)/shard_map/while/body/eval_jaxpr/ppermute | solution.py:12
  174.7 2.2 collective-permute-done
  176.9 1.5 select_select_fusion.2
  178.4 12.7 %collective-permute-start = (f32[128,1792]{1,0:T(8,128)}, f32[128,1792]{1,0:T(8,128)S(1)}, u32[]{:S(2)}, u32[]{:S(2)}) collective-permute-start(f32[128,1792]{1,0:T(8,128)} %get-tuple-element.455), channel_id=1, source_target_pairs={{0,32},{32,64},{64,96},{96,128},{128,160},{160,192},{192,224},{1,3... | collective-permute-start | bytes 2752520 | tf_op jit(solution)/shard_map/while/body/eval_jaxpr/ppermute | solution.py:12
  191.1 2.2 collective-permute-done
  194.9 12.7 %collective-permute-start = (f32[128,1792]{1,0:T(8,128)}, f32[128,1792]{1,0:T(8,128)S(1)}, u32[]{:S(2)}, u32[]{:S(2)}) collective-permute-start(f32[128,1792]{1,0:T(8,128)} %get-tuple-element.455), channel_id=1, source_target_pairs={{0,32},{32,64},{64,96},{96,128},{128,160},{160,192},{192,224},{1,3... | collective-permute-start | bytes 2752520 | tf_op jit(solution)/shard_map/while/body/eval_jaxpr/ppermute | solution.py:12
  207.6 2.2 collective-permute-done
  211.4 12.7 %collective-permute-start = (f32[128,1792]{1,0:T(8,128)}, f32[128,1792]{1,0:T(8,128)S(1)}, u32[]{:S(2)}, u32[]{:S(2)}) collective-permute-start(f32[128,1792]{1,0:T(8,128)} %get-tuple-element.455), channel_id=1, source_target_pairs={{0,32},{32,64},{64,96},{96,128},{128,160},{160,192},{192,224},{1,3... | collective-permute-start | bytes 2752520 | tf_op jit(solution)/shard_map/while/body/eval_jaxpr/ppermute | solution.py:12
  224.0 2.2 collective-permute-done
  227.8 12.7 %collective-permute-start = (f32[128,1792]{1,0:T(8,128)}, f32[128,1792]{1,0:T(8,128)S(1)}, u32[]{:S(2)}, u32[]{:S(2)}) collective-permute-start(f32[128,1792]{1,0:T(8,128)} %get-tuple-element.455), channel_id=1, source_target_pairs={{0,32},{32,64},{64,96},{96,128},{128,160},{160,192},{192,224},{1,3... | collective-permute-start | bytes 2752520 | tf_op jit(solution)/shard_map/while/body/eval_jaxpr/ppermute | solution.py:12
  240.5 2.2 collective-permute-done
  244.3 12.7 %collective-permute-start = (f32[128,1792]{1,0:T(8,128)}, f32[128,1792]{1,0:T(8,128)S(1)}, u32[]{:S(2)}, u32[]{:S(2)}) collective-permute-start(f32[128,1792]{1,0:T(8,128)} %get-tuple-element.455), channel_id=1, source_target_pairs={{0,32},{32,64},{64,96},{96,128},{128,160},{160,192},{192,224},{1,3... | collective-permute-start | bytes 2752520 | tf_op jit(solution)/shard_map/while/body/eval_jaxpr/ppermute | solution.py:12
  256.9 2.2 collective-permute-done
  260.7 12.7 %collective-permute-start = (f32[128,1792]{1,0:T(8,128)}, f32[128,1792]{1,0:T(8,128)S(1)}, u32[]{:S(2)}, u32[]{:S(2)}) collective-permute-start(f32[128,1792]{1,0:T(8,128)} %get-tuple-element.455), channel_id=1, source_target_pairs={{0,32},{32,64},{64,96},{96,128},{128,160},{160,192},{192,224},{1,3... | collective-permute-start | bytes 2752520 | tf_op jit(solution)/shard_map/while/body/eval_jaxpr/ppermute | solution.py:12
  273.4 2.2 collective-permute-done
  276.7 74.4 %all-reduce.2.cloned.1.call-done = f32[128,1792]{1,0:T(8,128)} async-done(((f32[128,1792]{1,0:T(8,128)}), f32[128,1792]{1,0:T(8,128)}) %all-reduce.2.cloned.1.call-update) | async-done | bytes 917520 | tf_op jit(solution)/shard_map/psum | solution.py:47
  351.1 8.4 %fusion.4 = (f32[128,1792]{1,0:T(8,128)S(1)}, f32[128,1792]{1,0:T(8,128)S(1)}, f32[128,1792]{1,0:T(8,128)}) fusion(f32[128,1792]{1,0:T(8,128)} %copy-done, f32[128,1792]{1,0:T(8,128)} %all-reduce.2.cloned.1.call-done, f32[1792]{0:T(1024)S(1)} %get-tuple-element.528, bf16[128,3584]{1,0:T(8,128)(2,1)} %param.8, ...), kind=kOutput, calls=%fused_computation.16 | convolution fusion | flops 1646231552 | bytes 18357248 | tf_op jit(solution)/shard_map/dot_general | solution.py:24
  359.4 99.1 %while.35 = (s32[]{:T(128)}, f32[128,1792]{1,0:T(8,128)}, f32[1792]{0:T(1024)S(1)}, f32[1792]{0:T(1024)S(1)}, f32[128,1792]{1,0:T(8,128)S(1)}, /*index=5*/f32[12...) while((s32[]{:T(128)}, f32[128,1792]{1,0:T(8,128)}, ...), condition=%wide.region_5.6_spmd.clone, body=%wide.region_3.5_spmd.clone.sunk | while | flops 4132359 | bytes 7376058 | solution.py:62
  361.3 2.5 collective-permute-done.1
  363.8 2.0 convert_element_type.22
  365.8 1.7 add_reduce_fusion.2
  368.8 5.9 collective-permute-done.1
  374.7 2.0 convert_element_type.22
  376.8 1.7 add_reduce_fusion.2
  379.8 8.6 %collective-permute-done.1 = bf16[128,1792]{1,0:T(8,128)(2,1)} collective-permute-done((bf16[128,1792]{1,0:T(8,128)(2,1)S(1)}, bf16[128,1792]{1,0:T(8,128)(2,1)}, u32[]{:S(2)}, u32[]{:S(2)}) %collective-permute-start.1) | collective-permute-done | bytes 458784 | tf_op jit(solution)/shard_map/while/body/eval_jaxpr/ppermute | solution.py:12
  388.4 2.0 convert_element_type.22
  390.4 1.7 add_reduce_fusion.2
  393.4 8.6 %collective-permute-done.1 = bf16[128,1792]{1,0:T(8,128)(2,1)} collective-permute-done((bf16[128,1792]{1,0:T(8,128)(2,1)S(1)}, bf16[128,1792]{1,0:T(8,128)(2,1)}, u32[]{:S(2)}, u32[]{:S(2)}) %collective-permute-start.1) | collective-permute-done | bytes 458784 | tf_op jit(solution)/shard_map/while/body/eval_jaxpr/ppermute | solution.py:12
  402.0 2.0 convert_element_type.22
  404.0 1.7 add_reduce_fusion.2
  407.0 8.6 %collective-permute-done.1 = bf16[128,1792]{1,0:T(8,128)(2,1)} collective-permute-done((bf16[128,1792]{1,0:T(8,128)(2,1)S(1)}, bf16[128,1792]{1,0:T(8,128)(2,1)}, u32[]{:S(2)}, u32[]{:S(2)}) %collective-permute-start.1) | collective-permute-done | bytes 458784 | tf_op jit(solution)/shard_map/while/body/eval_jaxpr/ppermute | solution.py:12
  415.6 2.0 convert_element_type.22
  417.6 1.7 add_reduce_fusion.2
  420.7 8.6 %collective-permute-done.1 = bf16[128,1792]{1,0:T(8,128)(2,1)} collective-permute-done((bf16[128,1792]{1,0:T(8,128)(2,1)S(1)}, bf16[128,1792]{1,0:T(8,128)(2,1)}, u32[]{:S(2)}, u32[]{:S(2)}) %collective-permute-start.1) | collective-permute-done | bytes 458784 | tf_op jit(solution)/shard_map/while/body/eval_jaxpr/ppermute | solution.py:12
  429.2 2.0 convert_element_type.22
  431.3 1.7 add_reduce_fusion.2
  434.3 8.6 %collective-permute-done.1 = bf16[128,1792]{1,0:T(8,128)(2,1)} collective-permute-done((bf16[128,1792]{1,0:T(8,128)(2,1)S(1)}, bf16[128,1792]{1,0:T(8,128)(2,1)}, u32[]{:S(2)}, u32[]{:S(2)}) %collective-permute-start.1) | collective-permute-done | bytes 458784 | tf_op jit(solution)/shard_map/while/body/eval_jaxpr/ppermute | solution.py:12
  442.9 2.0 convert_element_type.22
  444.9 1.7 add_reduce_fusion.2
  447.9 8.6 %collective-permute-done.1 = bf16[128,1792]{1,0:T(8,128)(2,1)} collective-permute-done((bf16[128,1792]{1,0:T(8,128)(2,1)S(1)}, bf16[128,1792]{1,0:T(8,128)(2,1)}, u32[]{:S(2)}, u32[]{:S(2)}) %collective-permute-start.1) | collective-permute-done | bytes 458784 | tf_op jit(solution)/shard_map/while/body/eval_jaxpr/ppermute | solution.py:12
  456.5 2.0 convert_element_type.22
  458.5 210.8 %psum.15 = f32[1792]{0:T(1024)} all-reduce(f32[1792]{0:T(1024)S(1)} %get-tuple-element.289), channel_id=1, replica_groups=mesh['tm'=8,'mp'=4,'tok'=8] {'tm','tok'}, use_global_device_ids=true, to_apply=%region_6.7 | all-reduce | flops 1792 | bytes 14336 | tf_op jit(solution)/shard_map/psum | solution.py:65
  (37 shorter events, 22.0 us)
Async XLA Ops:
  7.2 140.9 %all-gather.2.cloned.1.call-start = ((), (), s32[]{:S(2)}) async-start(), calls=%async_computation | async-start | bytes 13045760 | tf_op jit(solution)/shard_map/all_gather | solution.py:22
  7.9 343.2 %all-reduce.2.cloned.1.call-start = ((), (), s32[]{:S(2)}) async-start(), calls=%async_computation.1 | async-start | bytes 1835008 | tf_op jit(solution)/shard_map/psum | solution.py:47
  8.0 147.5 %copy-start.2 = (f32[1792]{0:T(1024)S(1)}, f32[1792]{0:T(1024)}, u32[]{:S(2)}) copy-start(f32[1792]{0:T(1024)} %param.11) | copy-start | bytes 21508
  157.1 4.5 collective-permute-start
  163.1 13.8 %collective-permute-start = (f32[128,1792]{1,0:T(8,128)}, f32[128,1792]{1,0:T(8,128)S(1)}, u32[]{:S(2)}, u32[]{:S(2)}) collective-permute-start(f32[128,1792]{1,0:T(8,128)} %get-tuple-element.455), channel_id=1, source_target_pairs={{0,32},{32,64},{64,96},{96,128},{128,160},{160,192},{192,224},{1,3... | collective-permute-start | bytes 2752520 | tf_op jit(solution)/shard_map/while/body/eval_jaxpr/ppermute | solution.py:12
  178.4 14.9 %collective-permute-start = (f32[128,1792]{1,0:T(8,128)}, f32[128,1792]{1,0:T(8,128)S(1)}, u32[]{:S(2)}, u32[]{:S(2)}) collective-permute-start(f32[128,1792]{1,0:T(8,128)} %get-tuple-element.455), channel_id=1, source_target_pairs={{0,32},{32,64},{64,96},{96,128},{128,160},{160,192},{192,224},{1,3... | collective-permute-start | bytes 2752520 | tf_op jit(solution)/shard_map/while/body/eval_jaxpr/ppermute | solution.py:12
  194.9 14.9 %collective-permute-start = (f32[128,1792]{1,0:T(8,128)}, f32[128,1792]{1,0:T(8,128)S(1)}, u32[]{:S(2)}, u32[]{:S(2)}) collective-permute-start(f32[128,1792]{1,0:T(8,128)} %get-tuple-element.455), channel_id=1, source_target_pairs={{0,32},{32,64},{64,96},{96,128},{128,160},{160,192},{192,224},{1,3... | collective-permute-start | bytes 2752520 | tf_op jit(solution)/shard_map/while/body/eval_jaxpr/ppermute | solution.py:12
  211.4 14.9 %collective-permute-start = (f32[128,1792]{1,0:T(8,128)}, f32[128,1792]{1,0:T(8,128)S(1)}, u32[]{:S(2)}, u32[]{:S(2)}) collective-permute-start(f32[128,1792]{1,0:T(8,128)} %get-tuple-element.455), channel_id=1, source_target_pairs={{0,32},{32,64},{64,96},{96,128},{128,160},{160,192},{192,224},{1,3... | collective-permute-start | bytes 2752520 | tf_op jit(solution)/shard_map/while/body/eval_jaxpr/ppermute | solution.py:12
  227.8 14.9 %collective-permute-start = (f32[128,1792]{1,0:T(8,128)}, f32[128,1792]{1,0:T(8,128)S(1)}, u32[]{:S(2)}, u32[]{:S(2)}) collective-permute-start(f32[128,1792]{1,0:T(8,128)} %get-tuple-element.455), channel_id=1, source_target_pairs={{0,32},{32,64},{64,96},{96,128},{128,160},{160,192},{192,224},{1,3... | collective-permute-start | bytes 2752520 | tf_op jit(solution)/shard_map/while/body/eval_jaxpr/ppermute | solution.py:12
  244.3 14.9 %collective-permute-start = (f32[128,1792]{1,0:T(8,128)}, f32[128,1792]{1,0:T(8,128)S(1)}, u32[]{:S(2)}, u32[]{:S(2)}) collective-permute-start(f32[128,1792]{1,0:T(8,128)} %get-tuple-element.455), channel_id=1, source_target_pairs={{0,32},{32,64},{64,96},{96,128},{128,160},{160,192},{192,224},{1,3... | collective-permute-start | bytes 2752520 | tf_op jit(solution)/shard_map/while/body/eval_jaxpr/ppermute | solution.py:12
  260.7 14.9 %collective-permute-start = (f32[128,1792]{1,0:T(8,128)}, f32[128,1792]{1,0:T(8,128)S(1)}, u32[]{:S(2)}, u32[]{:S(2)}) collective-permute-start(f32[128,1792]{1,0:T(8,128)} %get-tuple-element.455), channel_id=1, source_target_pairs={{0,32},{32,64},{64,96},{96,128},{128,160},{160,192},{192,224},{1,3... | collective-permute-start | bytes 2752520 | tf_op jit(solution)/shard_map/while/body/eval_jaxpr/ppermute | solution.py:12
  275.6 1.0 copy-start
  276.7 82.8 %copy-start.1 = (f32[128,1792]{1,0:T(8,128)S(1)}, f32[128,1792]{1,0:T(8,128)}, u32[]{:S(2)}) copy-start(f32[128,1792]{1,0:T(8,128)} %copy-done) | copy-start | bytes 2752516
  360.0 3.8 collective-permute-start.1
  367.5 7.2 %collective-permute-start.1 = (bf16[128,1792]{1,0:T(8,128)(2,1)S(1)}, bf16[128,1792]{1,0:T(8,128)(2,1)}, u32[]{:S(2)}, u32[]{:S(2)}) collective-permute-start(bf16[128,1792]{1,0:T(8,128)(2,1)S(1)} %get-tuple-element.465), channel_id=1, source_target_pairs={{32,0},{64,32},{96,64},{128,96},{160,128},{192,160},{224,192},{33,... | collective-permute-start | bytes 1376264 | tf_op jit(solution)/shard_map/while/body/eval_jaxpr/ppermute | solution.py:12
  378.5 9.9 %collective-permute-start.1 = (bf16[128,1792]{1,0:T(8,128)(2,1)S(1)}, bf16[128,1792]{1,0:T(8,128)(2,1)}, u32[]{:S(2)}, u32[]{:S(2)}) collective-permute-start(bf16[128,1792]{1,0:T(8,128)(2,1)S(1)} %get-tuple-element.465), channel_id=1, source_target_pairs={{32,0},{64,32},{96,64},{128,96},{160,128},{192,160},{224,192},{33,... | collective-permute-start | bytes 1376264 | tf_op jit(solution)/shard_map/while/body/eval_jaxpr/ppermute | solution.py:12
  392.1 9.9 %collective-permute-start.1 = (bf16[128,1792]{1,0:T(8,128)(2,1)S(1)}, bf16[128,1792]{1,0:T(8,128)(2,1)}, u32[]{:S(2)}, u32[]{:S(2)}) collective-permute-start(bf16[128,1792]{1,0:T(8,128)(2,1)S(1)} %get-tuple-element.465), channel_id=1, source_target_pairs={{32,0},{64,32},{96,64},{128,96},{160,128},{192,160},{224,192},{33,... | collective-permute-start | bytes 1376264 | tf_op jit(solution)/shard_map/while/body/eval_jaxpr/ppermute | solution.py:12
  405.7 9.9 %collective-permute-start.1 = (bf16[128,1792]{1,0:T(8,128)(2,1)S(1)}, bf16[128,1792]{1,0:T(8,128)(2,1)}, u32[]{:S(2)}, u32[]{:S(2)}) collective-permute-start(bf16[128,1792]{1,0:T(8,128)(2,1)S(1)} %get-tuple-element.465), channel_id=1, source_target_pairs={{32,0},{64,32},{96,64},{128,96},{160,128},{192,160},{224,192},{33,... | collective-permute-start | bytes 1376264 | tf_op jit(solution)/shard_map/while/body/eval_jaxpr/ppermute | solution.py:12
  419.3 9.9 %collective-permute-start.1 = (bf16[128,1792]{1,0:T(8,128)(2,1)S(1)}, bf16[128,1792]{1,0:T(8,128)(2,1)}, u32[]{:S(2)}, u32[]{:S(2)}) collective-permute-start(bf16[128,1792]{1,0:T(8,128)(2,1)S(1)} %get-tuple-element.465), channel_id=1, source_target_pairs={{32,0},{64,32},{96,64},{128,96},{160,128},{192,160},{224,192},{33,... | collective-permute-start | bytes 1376264 | tf_op jit(solution)/shard_map/while/body/eval_jaxpr/ppermute | solution.py:12
  433.0 9.9 %collective-permute-start.1 = (bf16[128,1792]{1,0:T(8,128)(2,1)S(1)}, bf16[128,1792]{1,0:T(8,128)(2,1)}, u32[]{:S(2)}, u32[]{:S(2)}) collective-permute-start(bf16[128,1792]{1,0:T(8,128)(2,1)S(1)} %get-tuple-element.465), channel_id=1, source_target_pairs={{32,0},{64,32},{96,64},{128,96},{160,128},{192,160},{224,192},{33,... | collective-permute-start | bytes 1376264 | tf_op jit(solution)/shard_map/while/body/eval_jaxpr/ppermute | solution.py:12
  446.6 9.9 %collective-permute-start.1 = (bf16[128,1792]{1,0:T(8,128)(2,1)S(1)}, bf16[128,1792]{1,0:T(8,128)(2,1)}, u32[]{:S(2)}, u32[]{:S(2)}) collective-permute-start(bf16[128,1792]{1,0:T(8,128)(2,1)S(1)} %get-tuple-element.465), channel_id=1, source_target_pairs={{32,0},{64,32},{96,64},{128,96},{160,128},{192,160},{224,192},{33,... | collective-permute-start | bytes 1376264 | tf_op jit(solution)/shard_map/while/body/eval_jaxpr/ppermute | solution.py:12
Sparse Core Ops, SparseCore 0:
  11.7 136.3 all-gather.1
  276.8 74.2 all-reduce.1
where the time goes:
time: 677 us; the launch traced here: 676 us
  waiting for transfers between devices  293 us (43%)
  blocking collectives  211 us (31%)
  starting transfers between devices  100 us (15%)
  other arithmetic  41 us (6%)
  matrix products  15.7 us (2%)
  between operations  14.1 us (2%)
    psum x1, blocking collectives, on_device(): grad_threshold = lax.psum(grad_local, ('tm', 'tok'))  211 us
    all_gather x1, waiting for transfers between devices, on_device(): piece = lax.all_gather(gate_weight, ('tm', 'tok'), axis=0, tiled=True)  140 us
    ppermute x16, starting transfers between devices, passed_along(): return lax.ppermute(x, axis, pairs)  100 us
    ppermute x16, waiting for transfers between devices, passed_along(): return lax.ppermute(x, axis, pairs)  77.7 us
    psum x1, waiting for transfers between devices, on_device(): total = lax.psum(spikes, 'tm')  74.4 us
    convert_element_type x8, other arithmetic, backward_turn(): passed_along((incoming + dwide).astype(jnp.bfloat16), 'tm', -1)  16.3 us
  transfers between devices with their start and end apart: 18, of which 18 were waited for; matrix products, arithmetic and copies ran while one was open for 0% of the time, Pallas kernels for 0%

commit v1 on v0

--- a/solution.py
+++ b/solution.py
@@ -44,7 +44,9 @@
     unused, spikes = lax.fori_loop(
         0, turns, forward_turn, (block_zero, jnp.zeros((rows, width), jnp.float32))
     )
-    total = lax.psum(spikes, "tm")
+    total = spikes
+    for hop in (1, 2, 4):
+        total = total + lax.ppermute(total, "tm", [(dev, dev ^ hop) for dev in range(8)])
     rates = threshold * total / steps
     error = (rates - target) / tokens_all
 

time: 677 us -> 654 us (0.966)
  waiting for transfers between devices: 293 us -> 257 us
  starting transfers between devices: 100 us -> 117 us
    psum x1 -> x0, waiting for transfers between devices: 74.4 us -> none  [on_device(): total = lax.psum(spikes, 'tm')]
    ppermute x0 -> x3, waiting for transfers between devices: none -> 36.2 us  [on_device(): lax.ppermute(total, 'tm', [(dev, dev ^ hop) for dev in range(8)])]
    ppermute x0 -> x3, starting transfers between devices: none -> 16.8 us  [on_device(): lax.ppermute(total, 'tm', [(dev, dev ^ hop) for dev in range(8)])]
  transfers between devices with their start and end apart: 18 -> 20, of which waited for: 18 -> 20; matrix products, arithmetic and copies ran while one was open for 0% -> 1% of each run, Pallas kernels for 0% -> 0%
where the time goes in v1:
time: 654 us; the launch traced here: 652 us
  waiting for transfers between devices  257 us (39%)
  blocking collectives  205 us (31%)
  starting transfers between devices  117 us (18%)
  other arithmetic  44.1 us (7%)
  matrix products  14.1 us (2%)
  between operations  14.1 us (2%)
    psum x1, blocking collectives, on_device(): grad_threshold = lax.psum(grad_local, ('tm', 'tok'))  205 us
    all_gather x1, waiting for transfers between devices, on_device(): piece = lax.all_gather(gate_weight, ('tm', 'tok'), axis=0, tiled=True)  140 us
    ppermute x16, starting transfers between devices, passed_along(): return lax.ppermute(x, axis, pairs)  100 us
    ppermute x16, waiting for transfers between devices, passed_along(): return lax.ppermute(x, axis, pairs)  79.7 us
    ppermute x3, waiting for transfers between devices, on_device(): lax.ppermute(total, 'tm', [(dev, dev ^ hop) for dev in range(8)])  36.2 us
    ppermute x3, starting transfers between devices, on_device(): lax.ppermute(total, 'tm', [(dev, dev ^ hop) for dev in range(8)])  16.8 us
    convert_element_type x8, other arithmetic, backward_turn(): passed_along((incoming + dwide).astype(jnp.bfloat16), 'tm', -1)  16.5 us
  transfers between devices with their start and end apart: 20, of which 20 were waited for; matrix products, arithmetic and copies ran while one was open for 1% of the time, Pallas kernels for 0%

profile of v1, /device:TPU:32, one launch (start us, length us, event | category | flops | bytes accessed | tf_op | source)
XLA Modules:
  0.0 652.0 jit_solution(9255586875958625832)
XLA Ops:
  7.9 140.1 %all-gather.2.cloned.1.call-done = bf16[3584,1792]{1,0:T(8,128)(2,1)} async-done(((bf16[56,1792]{1,0:T(8,128)(2,1)}), bf16[3584,1792]{1,0:T(8,128)(2,1)}) %all-gather.2.cloned.1.call-update) | async-done | bytes 12845072 | tf_op jit(solution)/shard_map/all_gather | solution.py:22
  148.0 7.4 %convolution_multiply_fusion = f32[128,1792]{1,0:T(8,128)S(1)} fusion(bf16[3584,1792]{1,0:T(8,128)(2,1)} %all-gather.2.cloned.1.call-done, bf16[128,3584]{1,0:T(8,128)(2,1)} %param.8, s32[1,128,3584]{2,1,0:T(8,128)} %param.9), kind=kOutput, calls=%fused_computation.8 | convolution fusion | flops 1645314048 | bytes 16515072 | tf_op jit(solution)/shard_map/dot_general | solution.py:23
  155.5 120.2 %while.34 = (s32[]{:T(128)}, f32[128,1792]{1,0:T(8,128)S(1)}, f32[128,1792]{1,0:T(8,128)S(1)}, f32[128,1792]{1,0:T(8,128)S(1)}, f32[1792]{0:T(1024)S(1)}, /*index=5*/s32[]{:T(128)}, s32[]{:T(128)}, s32[]{:T(128)}) while((s32[]{:T(128)}, f32[128,1792]{1,0:T(8,128)S(1)}, f32[128,1792]{1,0:T(8,128)S(1)}, f32[128,1792]{1,0:T(8,128)S(1)}, ...), condition=%wide.region_1.2_spmd.clone, body=%wide.region_0.1_spmd.clone.sunk | while | flops 2293767 | bytes 8264873 | solution.py:44
  157.1 2.2 collective-permute-start
  159.3 2.2 collective-permute-done
  163.1 11.6 %collective-permute-start = (f32[128,1792]{1,0:T(8,128)}, f32[128,1792]{1,0:T(8,128)S(1)}, u32[]{:S(2)}, u32[]{:S(2)}) collective-permute-start(f32[128,1792]{1,0:T(8,128)} %get-tuple-element.455), channel_id=1, source_target_pairs={{0,32},{32,64},{64,96},{96,128},{128,160},{160,192},{192,224},{1,3... | collective-permute-start | bytes 2752520 | tf_op jit(solution)/shard_map/while/body/eval_jaxpr/ppermute | solution.py:12
  174.7 2.2 collective-permute-done
  178.4 12.7 %collective-permute-start = (f32[128,1792]{1,0:T(8,128)}, f32[128,1792]{1,0:T(8,128)S(1)}, u32[]{:S(2)}, u32[]{:S(2)}) collective-permute-start(f32[128,1792]{1,0:T(8,128)} %get-tuple-element.455), channel_id=1, source_target_pairs={{0,32},{32,64},{64,96},{96,128},{128,160},{160,192},{192,224},{1,3... | collective-permute-start | bytes 2752520 | tf_op jit(solution)/shard_map/while/body/eval_jaxpr/ppermute | solution.py:12
  191.1 2.2 collective-permute-done
  194.9 12.7 %collective-permute-start = (f32[128,1792]{1,0:T(8,128)}, f32[128,1792]{1,0:T(8,128)S(1)}, u32[]{:S(2)}, u32[]{:S(2)}) collective-permute-start(f32[128,1792]{1,0:T(8,128)} %get-tuple-element.455), channel_id=1, source_target_pairs={{0,32},{32,64},{64,96},{96,128},{128,160},{160,192},{192,224},{1,3... | collective-permute-start | bytes 2752520 | tf_op jit(solution)/shard_map/while/body/eval_jaxpr/ppermute | solution.py:12
  207.6 2.2 collective-permute-done
  211.4 12.7 %collective-permute-start = (f32[128,1792]{1,0:T(8,128)}, f32[128,1792]{1,0:T(8,128)S(1)}, u32[]{:S(2)}, u32[]{:S(2)}) collective-permute-start(f32[128,1792]{1,0:T(8,128)} %get-tuple-element.455), channel_id=1, source_target_pairs={{0,32},{32,64},{64,96},{96,128},{128,160},{160,192},{192,224},{1,3... | collective-permute-start | bytes 2752520 | tf_op jit(solution)/shard_map/while/body/eval_jaxpr/ppermute | solution.py:12
  224.0 2.2 collective-permute-done
  227.8 12.7 %collective-permute-start = (f32[128,1792]{1,0:T(8,128)}, f32[128,1792]{1,0:T(8,128)S(1)}, u32[]{:S(2)}, u32[]{:S(2)}) collective-permute-start(f32[128,1792]{1,0:T(8,128)} %get-tuple-element.455), channel_id=1, source_target_pairs={{0,32},{32,64},{64,96},{96,128},{128,160},{160,192},{192,224},{1,3... | collective-permute-start | bytes 2752520 | tf_op jit(solution)/shard_map/while/body/eval_jaxpr/ppermute | solution.py:12
  240.5 2.2 collective-permute-done
  244.3 12.7 %collective-permute-start = (f32[128,1792]{1,0:T(8,128)}, f32[128,1792]{1,0:T(8,128)S(1)}, u32[]{:S(2)}, u32[]{:S(2)}) collective-permute-start(f32[128,1792]{1,0:T(8,128)} %get-tuple-element.455), channel_id=1, source_target_pairs={{0,32},{32,64},{64,96},{96,128},{128,160},{160,192},{192,224},{1,3... | collective-permute-start | bytes 2752520 | tf_op jit(solution)/shard_map/while/body/eval_jaxpr/ppermute | solution.py:12
  256.9 2.2 collective-permute-done
  260.7 12.7 %collective-permute-start = (f32[128,1792]{1,0:T(8,128)}, f32[128,1792]{1,0:T(8,128)S(1)}, u32[]{:S(2)}, u32[]{:S(2)}) collective-permute-start(f32[128,1792]{1,0:T(8,128)} %get-tuple-element.455), channel_id=1, source_target_pairs={{0,32},{32,64},{64,96},{96,128},{128,160},{160,192},{192,224},{1,3... | collective-permute-start | bytes 2752520 | tf_op jit(solution)/shard_map/while/body/eval_jaxpr/ppermute | solution.py:12
  273.4 2.2 collective-permute-done
  275.6 10.7 %collective-permute-start.2 = (f32[128,1792]{1,0:T(8,128)S(1)}, f32[128,1792]{1,0:T(8,128)S(1)}, u32[]{:S(2)}, u32[]{:S(2)}) collective-permute-start(f32[128,1792]{1,0:T(8,128)S(1)} %get-tuple-element.496), channel_id=1, source_target_pairs={{0,32},{32,0},{64,96},{96,64},{128,160},{160,128},{192,224},{224,1... | collective-permute-start | bytes 2752520 | tf_op jit(solution)/shard_map/ppermute | solution.py:49
  286.4 2.1 collective-permute-done.2
  288.6 2.7 collective-permute-start.3
  291.3 20.7 %collective-permute-done.3 = f32[128,1792]{1,0:T(8,128)S(1)} collective-permute-done((f32[128,1792]{1,0:T(8,128)S(1)}, f32[128,1792]{1,0:T(8,128)S(1)}, u32[]{:S(2)}, u32[]{:S(2)}) %collective-permute-start.3) | collective-permute-done | bytes 917536 | tf_op jit(solution)/shard_map/ppermute | solution.py:49
  312.0 3.4 collective-permute-start.4
  315.4 6.8 %fusion.5 = f32[128,1792]{1,0:T(8,128)S(1)} fusion(bf16[128,3584]{1,0:T(8,128)(2,1)} %param.8, bf16[3584,1792]{1,0:T(8,128)(2,1)} %all-gather.2.cloned.1.call-done), kind=kOutput, calls=%fused_computation.17 | convolution fusion | flops 1644167168 | bytes 14680064 | tf_op jit(solution)/shard_map/dot_general | solution.py:24
  322.2 13.4 %collective-permute-done.4 = f32[128,1792]{1,0:T(8,128)} collective-permute-done((f32[128,1792]{1,0:T(8,128)S(1)}, f32[128,1792]{1,0:T(8,128)}, u32[]{:S(2)}, u32[]{:S(2)}) %collective-permute-start.4) | collective-permute-done | bytes 917536 | tf_op jit(solution)/shard_map/ppermute | solution.py:49
  335.6 2.7 fusion.4
  338.3 101.3 %while.35 = (s32[]{:T(128)}, f32[128,1792]{1,0:T(8,128)}, f32[1792]{0:T(1024)S(1)}, f32[1792]{0:T(1024)S(1)}, f32[128,1792]{1,0:T(8,128)S(1)}, /*index=5*/f32[12...) while((s32[]{:T(128)}, f32[128,1792]{1,0:T(8,128)}, ...), condition=%wide.region_4.5_spmd.clone, body=%wide.region_2.4_spmd.clone.sunk | while | flops 4132359 | bytes 7376066 | solution.py:64
  340.2 2.5 collective-permute-done.1
  342.7 2.1 convert_element_type.22
  344.7 1.7 add_reduce_fusion.2
  347.7 7.9 %collective-permute-done.1 = bf16[128,1792]{1,0:T(8,128)(2,1)} collective-permute-done((bf16[128,1792]{1,0:T(8,128)(2,1)S(1)}, bf16[128,1792]{1,0:T(8,128)(2,1)}, u32[]{:S(2)}, u32[]{:S(2)}) %collective-permute-start.1) | collective-permute-done | bytes 458784 | tf_op jit(solution)/shard_map/while/body/eval_jaxpr/ppermute | solution.py:12
  355.6 2.1 convert_element_type.22
  360.7 8.6 %collective-permute-done.1 = bf16[128,1792]{1,0:T(8,128)(2,1)} collective-permute-done((bf16[128,1792]{1,0:T(8,128)(2,1)S(1)}, bf16[128,1792]{1,0:T(8,128)(2,1)}, u32[]{:S(2)}, u32[]{:S(2)}) %collective-permute-start.1) | collective-permute-done | bytes 458784 | tf_op jit(solution)/shard_map/while/body/eval_jaxpr/ppermute | solution.py:12
  369.3 2.1 convert_element_type.22
  371.4 1.7 add_reduce_fusion.2
  374.4 8.6 %collective-permute-done.1 = bf16[128,1792]{1,0:T(8,128)(2,1)} collective-permute-done((bf16[128,1792]{1,0:T(8,128)(2,1)S(1)}, bf16[128,1792]{1,0:T(8,128)(2,1)}, u32[]{:S(2)}, u32[]{:S(2)}) %collective-permute-start.1) | collective-permute-done | bytes 458784 | tf_op jit(solution)/shard_map/while/body/eval_jaxpr/ppermute | solution.py:12
  382.9 2.1 convert_element_type.22
  385.0 1.7 add_reduce_fusion.2
  388.0 8.6 %collective-permute-done.1 = bf16[128,1792]{1,0:T(8,128)(2,1)} collective-permute-done((bf16[128,1792]{1,0:T(8,128)(2,1)S(1)}, bf16[128,1792]{1,0:T(8,128)(2,1)}, u32[]{:S(2)}, u32[]{:S(2)}) %collective-permute-start.1) | collective-permute-done | bytes 458784 | tf_op jit(solution)/shard_map/while/body/eval_jaxpr/ppermute | solution.py:12
  396.6 2.1 convert_element_type.22
  401.7 8.6 %collective-permute-done.1 = bf16[128,1792]{1,0:T(8,128)(2,1)} collective-permute-done((bf16[128,1792]{1,0:T(8,128)(2,1)S(1)}, bf16[128,1792]{1,0:T(8,128)(2,1)}, u32[]{:S(2)}, u32[]{:S(2)}) %collective-permute-start.1) | collective-permute-done | bytes 458784 | tf_op jit(solution)/shard_map/while/body/eval_jaxpr/ppermute | solution.py:12
  410.3 2.1 convert_element_type.22
  415.3 8.6 %collective-permute-done.1 = bf16[128,1792]{1,0:T(8,128)(2,1)} collective-permute-done((bf16[128,1792]{1,0:T(8,128)(2,1)S(1)}, bf16[128,1792]{1,0:T(8,128)(2,1)}, u32[]{:S(2)}, u32[]{:S(2)}) %collective-permute-start.1) | collective-permute-done | bytes 458784 | tf_op jit(solution)/shard_map/while/body/eval_jaxpr/ppermute | solution.py:12
  423.9 2.1 convert_element_type.22
  429.0 8.6 %collective-permute-done.1 = bf16[128,1792]{1,0:T(8,128)(2,1)} collective-permute-done((bf16[128,1792]{1,0:T(8,128)(2,1)S(1)}, bf16[128,1792]{1,0:T(8,128)(2,1)}, u32[]{:S(2)}, u32[]{:S(2)}) %collective-permute-start.1) | collective-permute-done | bytes 458784 | tf_op jit(solution)/shard_map/while/body/eval_jaxpr/ppermute | solution.py:12
  437.6 2.1 convert_element_type.22
  439.6 205.5 %psum.7 = f32[1792]{0:T(1024)} all-reduce(f32[1792]{0:T(1024)S(1)} %get-tuple-element.289), channel_id=1, replica_groups=mesh['tm'=8,'mp'=4,'tok'=8] {'tm','tok'}, use_global_device_ids=true, to_apply=%region_5.6 | all-reduce | flops 1792 | bytes 14336 | tf_op jit(solution)/shard_map/psum | solution.py:67
  (41 shorter events, 31.0 us)
Async XLA Ops:
  7.2 140.9 %all-gather.2.cloned.1.call-start = ((), (), s32[]{:S(2)}) async-start(), calls=%async_computation | async-start | bytes 13045760 | tf_op jit(solution)/shard_map/all_gather | solution.py:22
  7.9 147.6 %copy-start.1 = (f32[1792]{0:T(1024)S(1)}, f32[1792]{0:T(1024)}, u32[]{:S(2)}) copy-start(f32[1792]{0:T(1024)} %param.11) | copy-start | bytes 21508
  157.1 4.5 collective-permute-start
  163.1 13.8 %collective-permute-start = (f32[128,1792]{1,0:T(8,128)}, f32[128,1792]{1,0:T(8,128)S(1)}, u32[]{:S(2)}, u32[]{:S(2)}) collective-permute-start(f32[128,1792]{1,0:T(8,128)} %get-tuple-element.455), channel_id=1, source_target_pairs={{0,32},{32,64},{64,96},{96,128},{128,160},{160,192},{192,224},{1,3... | collective-permute-start | bytes 2752520 | tf_op jit(solution)/shard_map/while/body/eval_jaxpr/ppermute | solution.py:12
  178.4 14.9 %collective-permute-start = (f32[128,1792]{1,0:T(8,128)}, f32[128,1792]{1,0:T(8,128)S(1)}, u32[]{:S(2)}, u32[]{:S(2)}) collective-permute-start(f32[128,1792]{1,0:T(8,128)} %get-tuple-element.455), channel_id=1, source_target_pairs={{0,32},{32,64},{64,96},{96,128},{128,160},{160,192},{192,224},{1,3... | collective-permute-start | bytes 2752520 | tf_op jit(solution)/shard_map/while/body/eval_jaxpr/ppermute | solution.py:12
  194.9 14.9 %collective-permute-start = (f32[128,1792]{1,0:T(8,128)}, f32[128,1792]{1,0:T(8,128)S(1)}, u32[]{:S(2)}, u32[]{:S(2)}) collective-permute-start(f32[128,1792]{1,0:T(8,128)} %get-tuple-element.455), channel_id=1, source_target_pairs={{0,32},{32,64},{64,96},{96,128},{128,160},{160,192},{192,224},{1,3... | collective-permute-start | bytes 2752520 | tf_op jit(solution)/shard_map/while/body/eval_jaxpr/ppermute | solution.py:12
  211.4 14.9 %collective-permute-start = (f32[128,1792]{1,0:T(8,128)}, f32[128,1792]{1,0:T(8,128)S(1)}, u32[]{:S(2)}, u32[]{:S(2)}) collective-permute-start(f32[128,1792]{1,0:T(8,128)} %get-tuple-element.455), channel_id=1, source_target_pairs={{0,32},{32,64},{64,96},{96,128},{128,160},{160,192},{192,224},{1,3... | collective-permute-start | bytes 2752520 | tf_op jit(solution)/shard_map/while/body/eval_jaxpr/ppermute | solution.py:12
  227.8 14.9 %collective-permute-start = (f32[128,1792]{1,0:T(8,128)}, f32[128,1792]{1,0:T(8,128)S(1)}, u32[]{:S(2)}, u32[]{:S(2)}) collective-permute-start(f32[128,1792]{1,0:T(8,128)} %get-tuple-element.455), channel_id=1, source_target_pairs={{0,32},{32,64},{64,96},{96,128},{128,160},{160,192},{192,224},{1,3... | collective-permute-start | bytes 2752520 | tf_op jit(solution)/shard_map/while/body/eval_jaxpr/ppermute | solution.py:12
  244.3 14.9 %collective-permute-start = (f32[128,1792]{1,0:T(8,128)}, f32[128,1792]{1,0:T(8,128)S(1)}, u32[]{:S(2)}, u32[]{:S(2)}) collective-permute-start(f32[128,1792]{1,0:T(8,128)} %get-tuple-element.455), channel_id=1, source_target_pairs={{0,32},{32,64},{64,96},{96,128},{128,160},{160,192},{192,224},{1,3... | collective-permute-start | bytes 2752520 | tf_op jit(solution)/shard_map/while/body/eval_jaxpr/ppermute | solution.py:12
  260.7 14.9 %collective-permute-start = (f32[128,1792]{1,0:T(8,128)}, f32[128,1792]{1,0:T(8,128)S(1)}, u32[]{:S(2)}, u32[]{:S(2)}) collective-permute-start(f32[128,1792]{1,0:T(8,128)} %get-tuple-element.455), channel_id=1, source_target_pairs={{0,32},{32,64},{64,96},{96,128},{128,160},{160,192},{192,224},{1,3... | collective-permute-start | bytes 2752520 | tf_op jit(solution)/shard_map/while/body/eval_jaxpr/ppermute | solution.py:12
  275.6 12.8 %collective-permute-start.2 = (f32[128,1792]{1,0:T(8,128)S(1)}, f32[128,1792]{1,0:T(8,128)S(1)}, u32[]{:S(2)}, u32[]{:S(2)}) collective-permute-start(f32[128,1792]{1,0:T(8,128)S(1)} %get-tuple-element.496), channel_id=1, source_target_pairs={{0,32},{32,0},{64,96},{96,64},{128,160},{160,128},{192,224},{224,1... | collective-permute-start | bytes 2752520 | tf_op jit(solution)/shard_map/ppermute | solution.py:49
  288.6 23.4 %collective-permute-start.3 = (f32[128,1792]{1,0:T(8,128)S(1)}, f32[128,1792]{1,0:T(8,128)S(1)}, u32[]{:S(2)}, u32[]{:S(2)}) collective-permute-start(f32[128,1792]{1,0:T(8,128)S(1)} %add.91), channel_id=1, source_target_pairs={{0,64},{32,96},{64,0},{96,32},{128,192},{160,224},{192,128},{224,1... | collective-permute-start | bytes 2752520 | tf_op jit(solution)/shard_map/ppermute | solution.py:49
  312.0 10.2 %copy-start = (f32[128,1792]{1,0:T(8,128)}, f32[128,1792]{1,0:T(8,128)S(1)}, u32[]{:S(2)}) copy-start(f32[128,1792]{1,0:T(8,128)S(1)} %add.92) | copy-start | bytes 2752516
  312.0 23.6 %collective-permute-start.4 = (f32[128,1792]{1,0:T(8,128)S(1)}, f32[128,1792]{1,0:T(8,128)}, u32[]{:S(2)}, u32[]{:S(2)}) collective-permute-start(f32[128,1792]{1,0:T(8,128)S(1)} %add.92), channel_id=1, source_target_pairs={{0,128},{32,160},{64,192},{96,224},{128,0},{160,32},{192,64},{224,... | collective-permute-start | bytes 2752520 | tf_op jit(solution)/shard_map/ppermute | solution.py:49
  338.8 3.8 collective-permute-start.1
  346.4 9.2 %collective-permute-start.1 = (bf16[128,1792]{1,0:T(8,128)(2,1)S(1)}, bf16[128,1792]{1,0:T(8,128)(2,1)}, u32[]{:S(2)}, u32[]{:S(2)}) collective-permute-start(bf16[128,1792]{1,0:T(8,128)(2,1)S(1)} %get-tuple-element.465), channel_id=1, source_target_pairs={{32,0},{64,32},{96,64},{128,96},{160,128},{192,160},{224,192},{33,... | collective-permute-start | bytes 1376264 | tf_op jit(solution)/shard_map/while/body/eval_jaxpr/ppermute | solution.py:12
  359.4 9.9 %collective-permute-start.1 = (bf16[128,1792]{1,0:T(8,128)(2,1)S(1)}, bf16[128,1792]{1,0:T(8,128)(2,1)}, u32[]{:S(2)}, u32[]{:S(2)}) collective-permute-start(bf16[128,1792]{1,0:T(8,128)(2,1)S(1)} %get-tuple-element.465), channel_id=1, source_target_pairs={{32,0},{64,32},{96,64},{128,96},{160,128},{192,160},{224,192},{33,... | collective-permute-start | bytes 1376264 | tf_op jit(solution)/shard_map/while/body/eval_jaxpr/ppermute | solution.py:12
  373.0 9.9 %collective-permute-start.1 = (bf16[128,1792]{1,0:T(8,128)(2,1)S(1)}, bf16[128,1792]{1,0:T(8,128)(2,1)}, u32[]{:S(2)}, u32[]{:S(2)}) collective-permute-start(bf16[128,1792]{1,0:T(8,128)(2,1)S(1)} %get-tuple-element.465), channel_id=1, source_target_pairs={{32,0},{64,32},{96,64},{128,96},{160,128},{192,160},{224,192},{33,... | collective-permute-start | bytes 1376264 | tf_op jit(solution)/shard_map/while/body/eval_jaxpr/ppermute | solution.py:12
  386.7 9.9 %collective-permute-start.1 = (bf16[128,1792]{1,0:T(8,128)(2,1)S(1)}, bf16[128,1792]{1,0:T(8,128)(2,1)}, u32[]{:S(2)}, u32[]{:S(2)}) collective-permute-start(bf16[128,1792]{1,0:T(8,128)(2,1)S(1)} %get-tuple-element.465), channel_id=1, source_target_pairs={{32,0},{64,32},{96,64},{128,96},{160,128},{192,160},{224,192},{33,... | collective-permute-start | bytes 1376264 | tf_op jit(solution)/shard_map/while/body/eval_jaxpr/ppermute | solution.py:12
  400.4 9.9 %collective-permute-start.1 = (bf16[128,1792]{1,0:T(8,128)(2,1)S(1)}, bf16[128,1792]{1,0:T(8,128)(2,1)}, u32[]{:S(2)}, u32[]{:S(2)}) collective-permute-start(bf16[128,1792]{1,0:T(8,128)(2,1)S(1)} %get-tuple-element.465), channel_id=1, source_target_pairs={{32,0},{64,32},{96,64},{128,96},{160,128},{192,160},{224,192},{33,... | collective-permute-start | bytes 1376264 | tf_op jit(solution)/shard_map/while/body/eval_jaxpr/ppermute | solution.py:12
  414.0 9.9 %collective-permute-start.1 = (bf16[128,1792]{1,0:T(8,128)(2,1)S(1)}, bf16[128,1792]{1,0:T(8,128)(2,1)}, u32[]{:S(2)}, u32[]{:S(2)}) collective-permute-start(bf16[128,1792]{1,0:T(8,128)(2,1)S(1)} %get-tuple-element.465), channel_id=1, source_target_pairs={{32,0},{64,32},{96,64},{128,96},{160,128},{192,160},{224,192},{33,... | collective-permute-start | bytes 1376264 | tf_op jit(solution)/shard_map/while/body/eval_jaxpr/ppermute | solution.py:12
  427.7 9.9 %collective-permute-start.1 = (bf16[128,1792]{1,0:T(8,128)(2,1)S(1)}, bf16[128,1792]{1,0:T(8,128)(2,1)}, u32[]{:S(2)}, u32[]{:S(2)}) collective-permute-start(bf16[128,1792]{1,0:T(8,128)(2,1)S(1)} %get-tuple-element.465), channel_id=1, source_target_pairs={{32,0},{64,32},{96,64},{128,96},{160,128},{192,160},{224,192},{33,... | collective-permute-start | bytes 1376264 | tf_op jit(solution)/shard_map/while/body/eval_jaxpr/ppermute | solution.py:12
Sparse Core Ops, SparseCore 0:
  11.7 136.3 all-gather.1
